TPU v7x, 128 devices: a whole 4x4x4 slice. The times are simulated.
128 devices in a mesh: sample: 32 (over x, z, core), feature: 4 (over y).
Axes of the slice: x: 4, y: 4, z: 4, core: 2. Of those that a mesh axis runs over, the one named last changes fastest.
Arguments:
- feat_values: float32 [65536, 2048], P('sample', 'feature'), may hold values from -0.6 to 0.6
- block_ids: int32 [512, 16], P('sample', 'feature'), may hold values from 0 to 8191
- fixed_weights: float32 [32768, 128], P('feature'), may hold values from -1.5 to 1.5
- labels: float32 [65536], P('sample'), may hold values from 0 to 1
- prior_scores: float32 [65536], P('sample'), may hold values from -3 to 3
- member_feats: float32 [65536, 128], P(('sample', 'feature')), may hold values from -1.8 to 1.8
- member_ids: int32 [65536], P(('sample', 'feature')), may hold values from 0 to 4095, as said below
- member_coefs: float32 [4096, 128], P(('sample', 'feature')), may hold values from -1.5 to 1.5
Outputs:
- new_weights: float32 [32768, 128], P('feature')
- new_coefs: float32 [4096, 128], P(('sample', 'feature'))
- total_scores: float32 [65536, 1], P(('sample', 'feature'))
Inputs may be any that keep to these rules, and one draw needn't show every extreme that they name: member_ids // 32 is the index along sample+feature of the device that owns the member; no member has more than 32 rows, and every member of some owner has exactly 32; at most 8 rows of one device belong to members of one owner, and every device has exactly 8 rows for some owner.
All inputs are finite; a program needn't handle non-finite values.
Results may differ from a plain program's by a relative error of at most 0.0003.
Values sent between devices are 32-bit elements; how exact they have to be, the bound alone decides.
No kernel may reach another device: no remote copies, remote signals or barrier semaphores. Data moves between devices by JAX's collectives and lax.ppermute only.
A program may use at most 128 MiB of HBM per device.

v0:
```python
import jax
import jax.numpy as jnp
from jax import lax
from jax.sharding import PartitionSpec as P

NEWTON = 2
STEP_SIZE = 0.5
FIXED_RIDGE = 0.1
MEMBER_RIDGE = 1.0
MEMBER_STEP = 0.5
HIGH = lax.Precision.HIGHEST


def partial_margin(tiled, block_ids, weights):
    chosen = weights[block_ids]
    local = jnp.einsum("trkb,tkb->tr", tiled, chosen, precision=HIGH).reshape(-1)
    return lax.psum(local, "feature")


def newton_update(weights, gradient, hessian):
    return weights - STEP_SIZE * (gradient + FIXED_RIDGE * weights) / (hessian + 1.0)


def member_solve(group_feats, weight, gradient_re):
    group = group_feats.shape[1]
    feat_width = group_feats.shape[2]
    scaled = group_feats * jnp.sqrt(weight)[:, :, None]
    small = (
        jnp.einsum("mgf,mhf->mgh", scaled, scaled, precision=HIGH)
        + MEMBER_RIDGE * jnp.eye(group, dtype=jnp.float32)[None]
    )
    projected = jnp.einsum("mgf,mf->mg", scaled, gradient_re, precision=HIGH)
    factor = jnp.linalg.cholesky(small)
    middle = lax.linalg.triangular_solve(factor, projected[:, :, None], left_side=True, lower=True)
    inner = lax.linalg.triangular_solve(
        factor, middle, left_side=True, lower=True, transpose_a=True
    )
    return gradient_re - jnp.einsum("mgf,mg->mf", scaled, inner[:, :, 0], precision=HIGH)


def shards(
    feat_values,
    block_ids,
    fixed_weights,
    labels,
    prior_scores,
    member_feats,
    member_ids,
    member_coefs,
):
    tile_count = block_ids.shape[0]
    slots_tile = block_ids.shape[1]
    block_width = fixed_weights.shape[1]
    shard_blocks = fixed_weights.shape[0]
    tiled = feat_values.reshape(tile_count, -1, slots_tile, block_width)
    margin = partial_margin(tiled, block_ids, fixed_weights)
    probs = jax.nn.sigmoid(margin + prior_scores)
    residual = (probs - labels).reshape(tile_count, -1)
    curvature = (probs * (1.0 - probs)).reshape(tile_count, -1)
    grad_tiles = jnp.einsum("trkb,tr->tkb", tiled, residual, precision=HIGH)
    hess_tiles = jnp.einsum("trkb,tr->tkb", tiled * tiled, curvature, precision=HIGH)
    stacked = jnp.stack([grad_tiles, hess_tiles]).reshape(2, -1, block_width)
    flat_ids = block_ids.reshape(-1)
    stats = jnp.zeros((2, shard_blocks, block_width), jnp.float32).at[:, flat_ids].add(stacked)
    totals = lax.psum(stats, "sample")
    new_weights = newton_update(fixed_weights, totals[0], totals[1])
    fixed_score = partial_margin(tiled, block_ids, new_weights)
    sample_count = lax.axis_size("sample")
    feature_count = lax.axis_size("feature")
    device_count = sample_count * feature_count
    rows_sample = labels.shape[0]
    send_rows = member_feats.shape[0]
    feat_width = member_feats.shape[1]
    member_count = member_coefs.shape[0]
    capacity = max(2, 2 * rows_sample // (feature_count * device_count))
    slot_total = device_count * capacity
    group = slot_total // member_count
    start_row = lax.axis_index("feature") * send_rows
    own_fixed = lax.dynamic_slice_in_dim(fixed_score, start_row, send_rows, 0)
    own_labels = lax.dynamic_slice_in_dim(labels, start_row, send_rows, 0)
    owner_of = member_ids // member_count
    row_range = jnp.arange(send_rows, dtype=jnp.int32)
    earlier = (owner_of[None, :] == owner_of[:, None]) & (row_range[None, :] < row_range[:, None])
    rank_owner = jnp.sum(earlier.astype(jnp.int32), axis=1)
    send_slots = owner_of * capacity + rank_owner
    local_member = jnp.remainder(member_ids, member_count).astype(jnp.float32)
    extras = jnp.stack([own_fixed, own_labels, local_member], axis=1)
    feat_buffer = jnp.zeros((slot_total, feat_width), jnp.float32).at[send_slots].set(member_feats)
    extra_buffer = (
        jnp.zeros((slot_total, 3), jnp.float32).at[:, 2].set(-1.0).at[send_slots].set(extras)
    )
    got_feats, got_extras = (
        lax.all_to_all(
            feat_buffer.reshape(device_count, capacity, feat_width),
            ("sample", "feature"),
            split_axis=0,
            concat_axis=0,
            tiled=True,
        ),
        lax.all_to_all(
            extra_buffer.reshape(device_count, capacity, 3),
            ("sample", "feature"),
            split_axis=0,
            concat_axis=0,
            tiled=True,
        ),
    )
    rows_feats = got_feats.reshape(slot_total, feat_width)
    rows_extra = got_extras.reshape(slot_total, 3)
    member_local = rows_extra[:, 2].astype(jnp.int32)
    sort_key = jnp.where(member_local >= 0, member_local, member_count)
    positions = jnp.arange(slot_total, dtype=jnp.int32)
    order = jnp.argsort(sort_key * slot_total + positions)
    sorted_member = sort_key[order]
    member_range = jnp.arange(member_count, dtype=jnp.int32)
    counts = jnp.sum((sort_key[:, None] == member_range[None, :]).astype(jnp.int32), axis=0)
    offsets = jnp.cumsum(counts) - counts
    clipped = jnp.minimum(sorted_member, member_count - 1)
    rank_in = positions - offsets[clipped]
    target = jnp.where(
        sorted_member < member_count, sorted_member * group + rank_in, member_count * group
    )
    grouped_rows = (
        jnp.full((member_count * group,), slot_total, jnp.int32).at[target].set(order, mode="drop")
    )
    padded_feats = jnp.concatenate([rows_feats, jnp.zeros((1, feat_width), jnp.float32)], axis=0)
    padded_extra = jnp.concatenate([rows_extra, jnp.zeros((1, 3), jnp.float32)], axis=0)
    group_feats = padded_feats[grouped_rows].reshape(member_count, group, feat_width)
    group_extra = padded_extra[grouped_rows].reshape(member_count, group, 3)
    live = (grouped_rows < slot_total).astype(jnp.float32).reshape(member_count, group)
    coefs = member_coefs
    for sweep in range(NEWTON):
        score = jnp.einsum("mgf,mf->mg", group_feats, coefs, precision=HIGH) + group_extra[:, :, 0]
        prob_now = jax.nn.sigmoid(score)
        error = (prob_now - group_extra[:, :, 1]) * live
        weight = prob_now * (1.0 - prob_now) * live
        gradient_re = (
            jnp.einsum("mgf,mg->mf", group_feats, error, precision=HIGH) + MEMBER_RIDGE * coefs
        )
        coefs = coefs - MEMBER_STEP * member_solve(group_feats, weight, gradient_re)
    group_final = jnp.einsum("mgf,mf->mg", group_feats, coefs, precision=HIGH) * live
    final = (
        jnp.zeros((slot_total + 1,), jnp.float32)
        .at[grouped_rows]
        .set(group_final.reshape(-1))[:slot_total]
    )
    returned = lax.all_to_all(
        final.reshape(device_count, capacity),
        ("sample", "feature"),
        split_axis=0,
        concat_axis=0,
        tiled=True,
    )
    member_score = returned.reshape(-1)[send_slots]
    total = own_fixed + member_score
    return (new_weights, coefs, total[:, None])


def solution(mesh):
    in_specs = (
        P("sample", "feature"),
        P("sample", "feature"),
        P("feature", None),
        P("sample"),
        P("sample"),
        P(("sample", "feature"), None),
        P(("sample", "feature")),
        P(("sample", "feature"), None),
    )
    out_specs = (P("feature", None), P(("sample", "feature"), None), P(("sample", "feature"), None))
    return jax.shard_map(shards, mesh=mesh, in_specs=in_specs, out_specs=out_specs, check_vma=False)
```

profile of v0, /device:TPU:1, one launch (start us, length us, event | category | flops | bytes accessed | tf_op | source)
XLA Modules:
  0.0 548.5 jit_solution(9729989409527750932)
XLA Ops:
  7.2 0.7 compare_select_fusion.7
  7.9 0.8 copy.89
  8.7 5.2 reshape.245
  14.1 6.7 %mul.86 = f32[16,128,4,128]{3,2,1,0:T(4,128)} multiply(f32[16,128,4,128]{3,2,1,0:T(4,128)} %reshape.245, f32[16,128,4,128]{3,2,1,0:T(4,128)} %reshape.245) | non-fusion elementwise | flops 1048576 | bytes 12582912 | tf_op jit(solution)/shard_map/mul | solution.py:61
  20.8 2.8 gather_fusion
  23.6 5.7 %fusion.6 = f32[16,1,128,1]{2,1,3,0:T(1,128)S(1)} fusion(f32[16,4,128,1]{2,3,1,0:T(1,128)S(1)} %bitcast.279, f32[16,128,4,128]{3,2,1,0:T(4,128)} %reshape.245), kind=kOutput, calls=%fused_computation.19 | convolution fusion | flops 12582912 | bytes 4235264 | tf_op jit(solution)/shard_map/trkb,tkb->tr/dot_general | solution.py:16
  29.3 9.7 %psum.21 = f32[2048]{0:T(1024)S(1)} all-reduce(f32[2048]{0:T(1024)S(1)} %bitcast.295), channel_id=1, replica_groups=mesh['sample'=32,'feature'=4] {'feature'}, use_global_device_ids=true, to_apply=%region_0.0 | all-reduce | flops 2048 | bytes 16384 | tf_op jit(solution)/shard_map/psum | solution.py:17
  39.0 4.3 fusion.2
  43.4 4.4 fusion
  47.9 5.5 %broadcast_in_dim.31 = f32[2,8192,128]{2,0,1:T(2,128)} broadcast(f32[]{:T(128)} %constant.124.clone.1), dimensions={} | broadcast | bytes 8388612 | tf_op jit(solution)/shard_map/broadcast_in_dim | solution.py:64
  53.4 6.7 %scatter_fusion = f32[2,8192,128]{2,0,1:T(2,128)} fusion(f32[2,8192,128]{2,0,1:T(2,128)} %broadcast_in_dim.31, s32[64]{0:T(128)S(1)} %fusion.52, f32[64,2,128]{2,1,0:T(2,128)S(1)} %maximum_bitcast_fusion), kind=kCustom, calls=%fused_computation.6 | custom fusion | flops 16384 | bytes 196864 | tf_op jit(solution)/shard_map/scatter-add | solution.py:64
  60.2 0.7 copy-done.5
  61.1 2.9 scatter_custom_fusion.1
  64.0 10.3 %all-to-all-start = ((f32[128,8,128]{2,1,0:T(8,128)}), f32[128,8,128]{2,1,0:T(8,128)S(1)}, u32[]{:S(2)}, u32[]{:S(2)}) async-start(f32[128,8,128]{2,1,0:T(8,128)} %bitcast.22), calls=%async_computation | async-start | bytes 1048576 | tf_op jit(solution)/shard_map/all_to_all | solution.py:93
  74.4 113.8 %all-reduce.4.cloned.1.call-done = f32[2,8192,128]{2,0,1:T(2,128)} async-done(((f32[2,8192,128]{2,0,1:T(2,128)}), f32[2,8192,128]{2,0,1:T(2,128)}) %all-reduce.4.cloned.1.call-update) | async-done | bytes 8388624 | tf_op jit(solution)/shard_map/psum | solution.py:65
  188.1 10.6 %fusion.54 = (f32[1,8192,128]{2,0,1:T(1,128)S(1)}, f32[1,8192,128]{2,0,1:T(1,128)S(1)}) fusion(f32[2,8192,128]{2,0,1:T(2,128)} %all-reduce.4.cloned.1.call-done), kind=kLoop, calls=%fused_computation.155 | loop fusion | flops 1048576 | bytes 16777216 | tf_op jit(solution)/shard_map/slice | solution.py:66
  198.8 2.8 divide_subtract_fusion
  201.6 2.8 gather_fusion.1
  204.4 5.7 %fusion.4 = f32[16,1,128,1]{2,1,3,0:T(1,128)S(1)} fusion(f32[16,4,128,1]{2,3,1,0:T(1,128)S(1)} %bitcast.278, f32[16,128,4,128]{3,2,1,0:T(4,128)} %reshape.245), kind=kOutput, calls=%fused_computation.17 | convolution fusion | flops 12582912 | bytes 4235264 | tf_op jit(solution)/shard_map/trkb,tkb->tr/dot_general | solution.py:16
  210.1 8.5 %psum.23 = f32[2048]{0:T(1024)S(1)} all-reduce(f32[2048]{0:T(1024)S(1)} %bitcast.294), channel_id=1, replica_groups=mesh['sample'=32,'feature'=4] {'feature'}, use_global_device_ids=true, to_apply=%region_5.6 | all-reduce | flops 2048 | bytes 16384 | tf_op jit(solution)/shard_map/psum | solution.py:17
  219.0 1.9 scatter_fusion.1
  220.9 1.5 copy.93
  222.4 7.5 %all-to-all-start.1 = ((f32[128,8,3]{1,2,0:T(4,128)}), f32[128,8,3]{1,2,0:T(4,128)S(1)}, u32[]{:S(2)}, u32[]{:S(2)}) async-start(f32[128,8,3]{1,2,0:T(4,128)} %copy.93), calls=%async_computation.1 | async-start | bytes 524288 | tf_op jit(solution)/shard_map/all_to_all | solution.py:100
  229.9 11.3 %all-to-all-done.1 = f32[128,8,3]{1,2,0:T(4,128)S(1)} async-done(((f32[128,8,3]{1,2,0:T(4,128)}), f32[128,8,3]{1,2,0:T(4,128)S(1)}, u32[]{:S(2)}, u32[]{:S(2)}) %all-to-all-start.1) | async-done | bytes 12320 | tf_op jit(solution)/shard_map/all_to_all | solution.py:100
  241.2 0.8 copy.94
  242.0 0.5 fusion.9
  242.9 0.7 fusion.57
  243.6 0.7 fusion.56
  244.4 4.4 sort.17
  248.8 4.5 gather_fusion.2
  253.6 3.5 compare_reduce_fusion.24
  257.1 4.7 select_reduce_fusion.2
  261.8 15.7 %select_select_fusion = s32[1024]{0:T(1024)S(1)} fusion(pred[1024]{0:T(1024)(128)(4,1)S(1)} %get-tuple-element.46, pred[1024]{0:T(1024)(128)(4,1)S(1)} %get-tuple-element.23, pred[1024]{0:T(1024)(128)(4,1)S(1)} %get-tuple-element.28, pred[1024]{0:T(1024)(128)(4,1)S(1)} %get-tuple-element.27, pred[1024]{0:T(1024)(128)(4,1)S(1)} %get-tuple-element.26, ...), kind=kLoop, calls=%fused_computation.132 | loop fusion | flops 25600 | bytes 33892 | tf_op jit(solution)/shard_map/gather | solution.py:119
  278.4 4.5 scatter_custom_fusion.3
  282.9 2.8 gather_fusion.4
  286.5 2.8 gather_fusion.3
  289.4 0.9 fusion.58
  290.4 0.6 fusion.59
  290.9 1.0 convolution_bitcast_fusion.5
  291.9 1.2 convolution_add_fusion.1
  293.4 93.8 %custom-call.12 = f32[32,32,32]{2,1,0:T(8,128)S(1)} custom-call(f32[32,32,32]{2,1,0:T(8,128)S(1)} %fusion.12), custom_call_target="Cholesky" | custom-call | tf_op jit(solution)/shard_map/jit(cholesky)/cholesky | solution.py:33
  388.0 12.5 %custom-call.14 = f32[32,1,32,32]{0,2,3,1:T(8,128)S(1)} custom-call(f32[32,1,32,32]{0,3,2,1:T(8,128)S(1)} %select_bitcast_fusion.1), custom_call_target="InvertDiagBlocksLowerTriangular" | custom-call | tf_op jit(solution)/shard_map/triangular_solve/custom-call.2 | solution.py:35
  400.4 0.4 copy.134
  400.9 0.6 convolution_bitcast_fusion.4
  401.5 0.9 convolution_bitcast_fusion.3
  402.4 0.7 fusion.18
  403.1 0.9 fusion.60
  404.0 0.6 fusion.61
  404.6 1.2 convolution_add_fusion
  405.8 1.0 convolution_bitcast_fusion.2
  407.1 93.8 %custom-call.15 = f32[32,32,32]{2,1,0:T(8,128)S(1)} custom-call(f32[32,32,32]{2,1,0:T(8,128)S(1)} %fusion.11), custom_call_target="Cholesky" | custom-call | tf_op jit(solution)/shard_map/jit(cholesky)/cholesky | solution.py:33
  501.6 12.7 %custom-call.17 = f32[32,1,32,32]{0,2,3,1:T(8,128)S(1)} custom-call(f32[32,1,32,32]{0,3,2,1:T(8,128)S(1)} %select_bitcast_fusion), custom_call_target="InvertDiagBlocksLowerTriangular" | custom-call | tf_op jit(solution)/shard_map/triangular_solve/custom-call.2 | solution.py:35
  514.8 0.6 convolution_bitcast_fusion.1
  515.4 0.9 convolution_bitcast_fusion
  516.3 0.7 fusion.14
  517.0 0.9 fusion.62
  518.0 4.3 scatter_custom_fusion.4
  522.4 0.7 all_to_all.14
  523.1 3.9 all-to-all-start.2
  527.0 9.9 %all-to-all-done.2 = f32[128,1,8]{2,1,0:T(1,128)S(1)} async-done(((f32[128,1,8]{2,1,0:T(1,128)}), f32[128,1,8]{2,1,0:T(1,128)S(1)}, u32[]{:S(2)}, u32[]{:S(2)}) %all-to-all-start.2) | async-done | bytes 4128 | tf_op jit(solution)/shard_map/all_to_all | solution.py:147
  536.8 0.5 broadcast.608
  537.4 0.8 reduce.68
  538.3 2.3 gather_fusion.5
  540.6 0.7 dynamic-slice_add_fusion
  (80 shorter events, 6.2 us)
Async XLA Ops:
  7.2 181.0 %all-reduce.4.cloned.1.call-start = ((), (), s32[]{:S(2)}) async-start(), calls=%async_computation.3 | async-start | bytes 16777216 | tf_op jit(solution)/shard_map/psum | solution.py:65
  20.8 18.2 %copy-start.3 = (f32[2048]{0:T(1024)S(1)}, f32[2048]{0:T(1024)}, u32[]{:S(2)}) copy-start(f32[2048]{0:T(1024)} %param.18) | copy-start | bytes 24580
  20.8 18.2 %copy-start.4 = (f32[2048]{0:T(1024)S(1)}, f32[2048]{0:T(1024)}, u32[]{:S(2)}) copy-start(f32[2048]{0:T(1024)} %param.19) | copy-start | bytes 24580
  60.1 0.7 copy-start.5
  64.0 158.4 %all-to-all-start = ((f32[128,8,128]{2,1,0:T(8,128)}), f32[128,8,128]{2,1,0:T(8,128)S(1)}, u32[]{:S(2)}, u32[]{:S(2)}) async-start(f32[128,8,128]{2,1,0:T(8,128)} %bitcast.22), calls=%async_computation | async-start | bytes 1048576 | tf_op jit(solution)/shard_map/all_to_all | solution.py:93
  188.1 10.6 %copy-start = (f32[8192,128]{1,0:T(8,128)S(1)}, f32[8192,128]{1,0:T(8,128)}, u32[]{:S(2)}) copy-start(f32[8192,128]{1,0:T(8,128)} %param.17) | copy-start | bytes 12582916
  201.6 17.3 %copy-start.6 = (f32[3]{0:T(128)S(1)}, f32[3]{0:T(128)}, u32[]{:S(2)}) copy-start(f32[3]{0:T(128)} %constant.136.clone.1) | copy-start | bytes 40
  222.4 18.8 %all-to-all-start.1 = ((f32[128,8,3]{1,2,0:T(4,128)}), f32[128,8,3]{1,2,0:T(4,128)S(1)}, u32[]{:S(2)}, u32[]{:S(2)}) async-start(f32[128,8,3]{1,2,0:T(4,128)} %copy.93), calls=%async_computation.1 | async-start | bytes 524288 | tf_op jit(solution)/shard_map/all_to_all | solution.py:100
  285.7 3.6 copy-start.1
  517.0 24.2 %copy-start.2 = (f32[32,128]{1,0:T(8,128)}, f32[32,128]{1,0:T(8,128)S(1)}, u32[]{:S(2)}) copy-start(f32[32,128]{1,0:T(8,128)S(1)} %multiply_subtract_fusion) | copy-start | bytes 49156
  523.1 13.8 %all-to-all-start.2 = ((f32[128,1,8]{2,1,0:T(1,128)}), f32[128,1,8]{2,1,0:T(1,128)S(1)}, u32[]{:S(2)}, u32[]{:S(2)}) async-start(f32[128,1,8]{2,1,0:T(1,128)} %bitcast.149), calls=%async_computation.2 | async-start | bytes 131072 | tf_op jit(solution)/shard_map/all_to_all | solution.py:147
Sparse Core Ops, SparseCore 0:
  60.3 127.7 all-reduce.3
where the time goes:
time: 558 us; the launch traced here: 549 us
  other arithmetic  273 us (49%)
  waiting for transfers between devices  135 us (24%)
  local copies, waits for them, and re-layouts  53.2 us (10%)
  matrix products  32.7 us (6%)
  starting transfers between devices  21.7 us (4%)
  blocking collectives  18.2 us (3%)
  between operations  15 us (3%)
    another operation x7, other arithmetic, member_solve(): factor = jnp.linalg.cholesky(small)  188 us
    psum x1, waiting for transfers between devices, shards(): totals = lax.psum(stats, 'sample')  114 us
    another operation x5, other arithmetic, member_solve(): lax.linalg.triangular_solve(factor, middle, left_side=True, lower=True, t...  25.6 us
    gather x3, other arithmetic, shards(): rank_in = positions - offsets[clipped]  23.9 us
    psum x2, blocking collectives, partial_margin(): return lax.psum(local, 'feature')  18.2 us
    dot_general x2, matrix products, partial_margin(): jnp.einsum('trkb,tkb->tr', tiled, chosen, precision=HIGH).reshape(-1)  11.4 us
    all_to_all x1, waiting for transfers between devices, shards(): lax.all_to_all(extra_buffer.reshape(device_count, capacity, 3), ('sample'...  11.3 us
  transfers between devices with their start and end apart: 4, of which 3 were waited for; matrix products, arithmetic and copies ran while one was open for 5% of the time, Pallas kernels for 0%

commit v1 on v0

--- a/solution.py
+++ b/solution.py
@@ -62,7 +62,11 @@
     stacked = jnp.stack([grad_tiles, hess_tiles]).reshape(2, -1, block_width)
     flat_ids = block_ids.reshape(-1)
     stats = jnp.zeros((2, shard_blocks, block_width), jnp.float32).at[:, flat_ids].add(stacked)
-    totals = lax.psum(stats, "sample")
+    size = lax.axis_size("sample")
+    totals, far = (stats, 1)
+    while far < size:
+        totals = totals + lax.ppermute(totals, "sample", [(i, i ^ far) for i in range(size)])
+        far = 2 * far
     new_weights = newton_update(fixed_weights, totals[0], totals[1])
     fixed_score = partial_margin(tiled, block_ids, new_weights)
     sample_count = lax.axis_size("sample")

time: 558 us -> 1190 us (2.13)
  waiting for transfers between devices: 135 us -> 740 us
  other arithmetic: 273 us -> 297 us
  starting transfers between devices: 21.7 us -> 39.8 us
  between operations: 15 us -> 1.41 us
    ppermute x0 -> x5, waiting for transfers between devices: none -> 719 us  [shards(): lax.ppermute(totals, 'sample', [(i, i ^ far) for i in range(size)])]
    psum x1 -> x0, waiting for transfers between devices: 114 us -> none  [shards(): totals = lax.psum(stats, 'sample')]
    add x0 -> x5, other arithmetic: none -> 27.6 us  [shards(): totals + lax.ppermute(totals, 'sample', [(i, i ^ far) for i in range(size)])]
  transfers between devices with their start and end apart: 4 -> 8, of which waited for: 3 -> 7; matrix products, arithmetic and copies ran while one was open for 5% -> 3% of each run, Pallas kernels for 0% -> 0%
where the time goes in v1:
time: 1190 us; the launch traced here: 1180 us
  waiting for transfers between devices  740 us (62%)
  other arithmetic  297 us (25%)
  local copies, waits for them, and re-layouts  52.5 us (4%)
  starting transfers between devices  39.8 us (3%)
  matrix products  32.7 us (3%)
  blocking collectives  15.7 us (1%)
    ppermute x5, waiting for transfers between devices, shards(): lax.ppermute(totals, 'sample', [(i, i ^ far) for i in range(size)])  719 us
    another operation x7, other arithmetic, member_solve(): factor = jnp.linalg.cholesky(small)  188 us
    add x5, other arithmetic, shards(): totals + lax.ppermute(totals, 'sample', [(i, i ^ far) for i in range(size)])  27.6 us
    another operation x5, other arithmetic, member_solve(): lax.linalg.triangular_solve(factor, middle, left_side=True, lower=True, t...  25.8 us
    gather x3, other arithmetic, shards(): rank_in = positions - offsets[clipped]  23.9 us
  transfers between devices with their start and end apart: 8, of which 7 were waited for; matrix products, arithmetic and copies ran while one was open for 3% of the time, Pallas kernels for 0%

profile of v1, /device:TPU:1, one launch (start us, length us, event | category | flops | bytes accessed | tf_op | source)
XLA Modules:
  0.0 1178.8 jit_solution(17018707260870122470)
XLA Ops:
  1.3 0.8 copy.89
  2.1 5.2 reshape.245
  7.5 6.7 mul.86
  14.2 2.8 gather_fusion
  17.1 5.7 fusion.6
  22.8 9.7 psum.14
  32.5 4.3 fusion.2
  36.9 4.4 fusion
  41.4 5.4 broadcast_in_dim.31
  46.8 6.7 scatter_fusion
  53.4 2.7 collective-permute-start
  56.1 13.0 %collective-permute-done = f32[2,8192,128]{2,0,1:T(2,128)S(1)} collective-permute-done((f32[2,8192,128]{2,0,1:T(2,128)}, f32[2,8192,128]{2,0,1:T(2,128)S(1)}, u32[]{:S(2)}, u32[]{:S(2)}) %collective-permute-start) | collective-permute-done | bytes 8388640 | tf_op jit(solution)/shard_map/ppermute | solution.py:68
  69.1 6.1 add.173
  75.2 1.7 collective-permute-start.1
  76.9 180.4 %collective-permute-done.1 = f32[2,8192,128]{2,0,1:T(2,128)S(1)} collective-permute-done((f32[2,8192,128]{2,0,1:T(2,128)S(1)}, f32[2,8192,128]{2,0,1:T(2,128)S(1)}, u32[]{:S(2)}, u32[]{:S(2)}) %collective-permute-start.1) | collective-permute-done | bytes 8388640 | tf_op jit(solution)/shard_map/ppermute | solution.py:68
  257.4 4.4 add.174
  261.8 3.4 collective-permute-start.2
  265.2 179.6 %collective-permute-done.2 = f32[2,8192,128]{2,0,1:T(2,128)S(1)} collective-permute-done((f32[2,8192,128]{2,0,1:T(2,128)S(1)}, f32[2,8192,128]{2,0,1:T(2,128)S(1)}, u32[]{:S(2)}, u32[]{:S(2)}) %collective-permute-start.2) | collective-permute-done | bytes 8388640 | tf_op jit(solution)/shard_map/ppermute | solution.py:68
  444.8 4.4 add.175
  449.2 1.3 collective-permute-start.3
  450.6 178.9 %collective-permute-done.3 = f32[2,8192,128]{2,0,1:T(2,128)S(1)} collective-permute-done((f32[2,8192,128]{2,0,1:T(2,128)S(1)}, f32[2,8192,128]{2,0,1:T(2,128)S(1)}, u32[]{:S(2)}, u32[]{:S(2)}) %collective-permute-start.3) | collective-permute-done | bytes 8388640 | tf_op jit(solution)/shard_map/ppermute | solution.py:68
  629.4 5.4 add.176
  634.9 2.7 collective-permute-start.4
  637.9 2.9 scatter_custom_fusion.1
  640.8 7.9 all-to-all-start
  648.8 167.2 %collective-permute-done.4 = f32[2,8192,128]{2,0,1:T(2,128)} collective-permute-done((f32[2,8192,128]{2,0,1:T(2,128)}, f32[2,8192,128]{2,0,1:T(2,128)}, u32[]{:S(2)}, u32[]{:S(2)}) %collective-permute-start.4) | collective-permute-done | bytes 8388640 | tf_op jit(solution)/shard_map/ppermute | solution.py:68
  815.9 7.2 add.177
  823.2 6.6 fusion.54
  829.8 2.8 divide_subtract_fusion
  832.7 2.8 gather_fusion.1
  835.5 5.7 fusion.4
  841.2 6.1 psum.15
  847.6 1.9 scatter_fusion.1
  849.5 1.5 copy.93
  851.0 16.2 %all-to-all-start.1 = ((f32[128,8,3]{1,2,0:T(4,128)}), f32[128,8,3]{1,2,0:T(4,128)S(1)}, u32[]{:S(2)}, u32[]{:S(2)}) async-start(f32[128,8,3]{1,2,0:T(4,128)} %copy.93), calls=%async_computation.1 | async-start | bytes 524288 | tf_op jit(solution)/shard_map/all_to_all | solution.py:104
  867.2 11.1 all-to-all-done.1
  878.4 0.8 copy.94
  880.8 0.7 fusion.56
  881.6 4.4 sort.17
  886.0 4.5 gather_fusion.2
  890.8 3.5 compare_reduce_fusion.24
  894.3 4.7 select_reduce_fusion.2
  899.0 15.7 %select_select_fusion = s32[1024]{0:T(1024)S(1)} fusion(pred[1024]{0:T(1024)(128)(4,1)S(1)} %get-tuple-element.46, pred[1024]{0:T(1024)(128)(4,1)S(1)} %get-tuple-element.23, pred[1024]{0:T(1024)(128)(4,1)S(1)} %get-tuple-element.28, pred[1024]{0:T(1024)(128)(4,1)S(1)} %get-tuple-element.27, pred[1024]{0:T(1024)(128)(4,1)S(1)} %get-tuple-element.26, ...), kind=kLoop, calls=%fused_computation.132 | loop fusion | flops 25600 | bytes 33892 | tf_op jit(solution)/shard_map/gather | solution.py:123
  915.6 4.6 scatter_custom_fusion.3
  920.2 2.8 gather_fusion.4
  923.7 2.8 gather_fusion.3
  926.6 0.9 fusion.58
  928.2 1.0 convolution_bitcast_fusion.5
  929.2 1.2 convolution_add_fusion.1
  930.7 93.8 %custom-call.12 = f32[32,32,32]{2,1,0:T(8,128)S(1)} custom-call(f32[32,32,32]{2,1,0:T(8,128)S(1)} %fusion.12), custom_call_target="Cholesky" | custom-call | tf_op jit(solution)/shard_map/jit(cholesky)/cholesky | solution.py:33
  1025.2 12.5 %custom-call.14 = f32[32,1,32,32]{0,2,3,1:T(8,128)S(1)} custom-call(f32[32,1,32,32]{0,3,2,1:T(8,128)S(1)} %select_bitcast_fusion.1), custom_call_target="InvertDiagBlocksLowerTriangular" | custom-call | tf_op jit(solution)/shard_map/triangular_solve/custom-call.2 | solution.py:35
  1038.7 0.9 convolution_bitcast_fusion.3
  1040.3 0.9 fusion.60
  1041.9 1.2 convolution_add_fusion
  1043.0 1.0 convolution_bitcast_fusion.2
  1044.3 93.8 %custom-call.15 = f32[32,32,32]{2,1,0:T(8,128)S(1)} custom-call(f32[32,32,32]{2,1,0:T(8,128)S(1)} %fusion.11), custom_call_target="Cholesky" | custom-call | tf_op jit(solution)/shard_map/jit(cholesky)/cholesky | solution.py:33
  1138.9 12.9 %custom-call.17 = f32[32,1,32,32]{0,2,3,1:T(8,128)S(1)} custom-call(f32[32,1,32,32]{0,3,2,1:T(8,128)S(1)} %select_bitcast_fusion), custom_call_target="InvertDiagBlocksLowerTriangular" | custom-call | tf_op jit(solution)/shard_map/triangular_solve/custom-call.2 | solution.py:35
  1152.8 0.9 convolution_bitcast_fusion
  1154.5 0.9 fusion.62
  1155.5 4.3 scatter_custom_fusion.4
  1160.5 3.9 all-to-all-start.2
  1164.4 9.9 all-to-all-done.2
  1174.8 0.8 reduce.68
  1175.7 2.3 gather_fusion.5
  (92 shorter events, 14.0 us)
Async XLA Ops:
  14.2 18.2 %copy-start.3 = (f32[2048]{0:T(1024)S(1)}, f32[2048]{0:T(1024)}, u32[]{:S(2)}) copy-start(f32[2048]{0:T(1024)} %param.18) | copy-start | bytes 24580
  14.2 18.2 %copy-start.4 = (f32[2048]{0:T(1024)S(1)}, f32[2048]{0:T(1024)}, u32[]{:S(2)}) copy-start(f32[2048]{0:T(1024)} %param.19) | copy-start | bytes 24580
  53.4 15.7 %collective-permute-start = (f32[2,8192,128]{2,0,1:T(2,128)}, f32[2,8192,128]{2,0,1:T(2,128)S(1)}, u32[]{:S(2)}, u32[]{:S(2)}) collective-permute-start(f32[2,8192,128]{2,0,1:T(2,128)} %scatter_fusion), channel_id=1, source_target_pairs={{0,4},{4,0},{8,12},{12,8},{16,20},{20,16},{24,28},{28,24},{32,36},... | collective-permute-start | bytes 25165832 | tf_op jit(solution)/shard_map/ppermute | solution.py:68
  75.2 182.2 %collective-permute-start.1 = (f32[2,8192,128]{2,0,1:T(2,128)S(1)}, f32[2,8192,128]{2,0,1:T(2,128)S(1)}, u32[]{:S(2)}, u32[]{:S(2)}) collective-permute-start(f32[2,8192,128]{2,0,1:T(2,128)S(1)} %add.173), channel_id=1, source_target_pairs={{0,8},{4,12},{8,0},{12,4},{16,24},{20,28},{24,16},{28,20},{32,40},... | collective-permute-start | bytes 25165832 | tf_op jit(solution)/shard_map/ppermute | solution.py:68
  261.8 183.0 %collective-permute-start.2 = (f32[2,8192,128]{2,0,1:T(2,128)S(1)}, f32[2,8192,128]{2,0,1:T(2,128)S(1)}, u32[]{:S(2)}, u32[]{:S(2)}) collective-permute-start(f32[2,8192,128]{2,0,1:T(2,128)S(1)} %add.174), channel_id=1, source_target_pairs={{0,16},{4,20},{8,24},{12,28},{16,0},{20,4},{24,8},{28,12},{32,48},... | collective-permute-start | bytes 25165832 | tf_op jit(solution)/shard_map/ppermute | solution.py:68
  449.2 188.4 %copy-start.5 = (s32[512]{0:T(512)S(1)}, s32[512]{0:T(512)}, u32[]{:S(2)}) copy-start(s32[512]{0:T(512)} %param.21) | copy-start | bytes 6148
  449.2 180.2 %collective-permute-start.3 = (f32[2,8192,128]{2,0,1:T(2,128)S(1)}, f32[2,8192,128]{2,0,1:T(2,128)S(1)}, u32[]{:S(2)}, u32[]{:S(2)}) collective-permute-start(f32[2,8192,128]{2,0,1:T(2,128)S(1)} %add.175), channel_id=1, source_target_pairs={{0,32},{4,36},{8,40},{12,44},{16,48},{20,52},{24,56},{28,60},{32,0... | collective-permute-start | bytes 25165832 | tf_op jit(solution)/shard_map/ppermute | solution.py:68
  634.9 181.1 %collective-permute-start.4 = (f32[2,8192,128]{2,0,1:T(2,128)}, f32[2,8192,128]{2,0,1:T(2,128)}, u32[]{:S(2)}, u32[]{:S(2)}) collective-permute-start(f32[2,8192,128]{2,0,1:T(2,128)} %add.176), channel_id=1, source_target_pairs={{0,64},{4,68},{8,72},{12,76},{16,80},{20,84},{24,88},{28,92},{32,9... | collective-permute-start | bytes 25165832 | tf_op jit(solution)/shard_map/ppermute | solution.py:68
  640.8 210.3 %all-to-all-start = ((f32[128,8,128]{2,1,0:T(8,128)}), f32[128,8,128]{2,1,0:T(8,128)S(1)}, u32[]{:S(2)}, u32[]{:S(2)}) async-start(f32[128,8,128]{2,1,0:T(8,128)} %bitcast.22), calls=%async_computation | async-start | bytes 1048576 | tf_op jit(solution)/shard_map/all_to_all | solution.py:97
  823.2 6.6 copy-start
  832.7 14.9 %copy-start.6 = (f32[3]{0:T(128)S(1)}, f32[3]{0:T(128)}, u32[]{:S(2)}) copy-start(f32[3]{0:T(128)} %constant.136.clone.1) | copy-start | bytes 40
  851.0 27.4 %all-to-all-start.1 = ((f32[128,8,3]{1,2,0:T(4,128)}), f32[128,8,3]{1,2,0:T(4,128)S(1)}, u32[]{:S(2)}, u32[]{:S(2)}) async-start(f32[128,8,3]{1,2,0:T(4,128)} %copy.93), calls=%async_computation.1 | async-start | bytes 524288 | tf_op jit(solution)/shard_map/all_to_all | solution.py:104
  923.0 3.6 copy-start.1
  1154.5 24.2 %copy-start.2 = (f32[32,128]{1,0:T(8,128)}, f32[32,128]{1,0:T(8,128)S(1)}, u32[]{:S(2)}) copy-start(f32[32,128]{1,0:T(8,128)S(1)} %multiply_subtract_fusion) | copy-start | bytes 49156
  1160.5 13.8 %all-to-all-start.2 = ((f32[128,1,8]{2,1,0:T(1,128)}), f32[128,1,8]{2,1,0:T(1,128)S(1)}, u32[]{:S(2)}, u32[]{:S(2)}) async-start(f32[128,1,8]{2,1,0:T(1,128)} %bitcast.149), calls=%async_computation.2 | async-start | bytes 131072 | tf_op jit(solution)/shard_map/all_to_all | solution.py:151
